TPU v7x, 256 devices: a whole 4x4x8 slice. The times are simulated.
256 devices in a mesh: grid: 32 (over y_hi, z, core), chan: 8 (over x, y_lo).
Axes of the slice: x: 4, y: 4 (y_hi: 2, y_lo: 2; y = y_hi * 2 + y_lo), z: 8, core: 2. Of those that a mesh axis runs over, the one named last changes fastest.
Arguments:
- activations: bfloat16 [256, 32, 8, 16, 128], P('chan', 'grid'), may hold values from -6 to 6
- grad_out: bfloat16 [256, 32, 16, 128], P('chan', 'grid'), may hold values from -6 to 6
- weight: bfloat16 [27, 256, 256], P(None, 'chan'), may hold values from -0.078125 to 0.078125
Outputs:
- grad_act: bfloat16 [256, 32, 8, 16, 128], P('chan', 'grid')
- grad_weight: float32 [27, 256, 256], P(None, 'chan')
All inputs are finite; a program needn't handle non-finite values.
Results may differ from a plain program's by a relative error of at most 0.001.
Values may be sent and summed in bfloat16 or wider, within the bound.
A program may use at most 64 MiB of HBM per device.

v0:
```python
import math
import jax
import jax.numpy as jnp
from jax import lax
from jax.sharding import PartitionSpec as P


def shifted_2(block, axis, distance):
    devices = range(lax.axis_size(axis))
    route = [(i - distance, i) for i in devices if i - distance in devices]
    return lax.ppermute(block, axis, route)


def parity_taps(parity):
    if parity == 0:
        return [(1, 0)]
    return [(2, 0), (0, 1)]


def tap_parity(tap):
    if tap == 1:
        return (0, 0)
    if tap == 2:
        return (1, 0)
    return (1, 1)


def shifted_grads(grad_cells, rim_plane):
    result = {}
    for step_x in range(2):
        if step_x == 0:
            x_shifted = grad_cells
        else:
            x_shifted = jnp.concatenate([grad_cells[:, 1:], rim_plane[:, None]], 1)
        for step_y in range(2):
            if step_y == 0:
                y_shifted = x_shifted
            else:
                y_shifted = jnp.concatenate(
                    [x_shifted[:, :, 1:], jnp.zeros_like(x_shifted[:, :, :1])], 2
                )
            for step_z in range(2):
                if step_z == 0:
                    z_shifted = y_shifted
                else:
                    z_shifted = jnp.concatenate(
                        [y_shifted[:, :, :, 1:], jnp.zeros_like(y_shifted[:, :, :, :1])], 3
                    )
                result[step_x, step_y, step_z] = z_shifted
    return result


def on_device(activations, grad_out, weight):
    cin_dev, planes, parities, out_y, out_z = activations.shape
    count_out = planes * out_y * out_z
    scale_norm = 1.0 / math.sqrt(count_out * lax.axis_size("grid"))
    front_plane = shifted_2(activations[:, planes - 1 : planes, 4:8], "grid", 1)
    act_before = jnp.concatenate([front_plane, activations[:, : planes - 1, 4:8]], 1)
    gathered = lax.all_gather(grad_out, "chan", axis=0, tiled=True)
    rim_whole = shifted_2(gathered[:, 0], "grid", -1)
    piece_rows = gathered.shape[0]
    shifted = shifted_grads(gathered, rim_whole)
    blocks = []
    for parity in range(8):
        par_x, par_y, par_z = (parity // 4, parity // 2 % 2, parity % 2)
        block_sum = jnp.zeros((cin_dev, count_out), jnp.float32)
        for tap_x, step_x in parity_taps(par_x):
            for tap_y, step_y in parity_taps(par_y):
                for tap_z, step_z in parity_taps(par_z):
                    window = shifted[step_x, step_y, step_z].reshape(piece_rows, count_out)
                    block_sum = block_sum + jnp.dot(
                        weight[tap_x * 9 + tap_y * 3 + tap_z],
                        window,
                        preferred_element_type=jnp.float32,
                    )
        blocks.append(block_sum.reshape(cin_dev, planes, out_y, out_z))
    totals = jnp.stack(blocks, 2)
    tap_list = []
    for tap_index in range(27):
        tap_x = tap_index // 9
        par_x, step_x = tap_parity(tap_x)
        par_y, step_y = tap_parity(tap_index // 3 % 3)
        par_z, step_z = tap_parity(tap_index % 3)
        par_index = 4 * par_x + 2 * par_y + par_z
        if tap_x == 0:
            act_slab = act_before[:, :, par_index - 4]
            grad_slab = shifted[0, step_y, step_z]
        else:
            act_slab = activations[:, :, par_index]
            grad_slab = shifted[step_x, step_y, step_z]
        tap_list.append(
            jnp.einsum("cxyz,oxyz->co", act_slab, grad_slab, preferred_element_type=jnp.float32)
        )
    tap_terms = jnp.stack(tap_list, 0)
    grad_w = tap_terms
    totals, grad_w = (totals, grad_w)
    grad_act = totals.astype(jnp.bfloat16)
    grad_weight = lax.psum(grad_w, "grid") * scale_norm
    return (grad_act, grad_weight)


def solution(mesh):
    placed = (
        P("chan", "grid", None, None, None),
        P("chan", "grid", None, None),
        P(None, "chan", None),
    )
    return jax.shard_map(
        on_device,
        mesh=mesh,
        in_specs=placed,
        out_specs=(P("chan", "grid", None, None, None), P(None, "chan", None)),
        check_vma=False,
    )
```

profile of v0, /device:TPU:1, one launch (start us, length us, event | category | flops | bytes accessed | tf_op | source)
XLA Modules:
  0.0 415.9 jit_solution(3259047934980850593)
XLA Ops:
  7.2 1.6 copy.16
  9.9 1.1 copy.42
  11.0 4.9 %collective-permute-start.1 = (bf16[32,1,4,16,128]{4,0,3,2,1:T(8,128)(2,1)}, bf16[32,1,4,16,128]{4,0,3,2,1:T(8,128)(2,1)}, u32[]{:S(2)}, u32[]{:S(2)}) collective-permute-start(bf16[32,1,4,16,128]{4,0,3,2,1:T(8,128)(2,1)} %copy.42), channel_id=1, source_target_pairs={{0,8},{8,16},{16,24},{24,32},{32,40},{40,48},{48,56},{56,64},{64,7... | collective-permute-start | bytes 1572872 | tf_op jit(solution)/shard_map/ppermute | solution.py:11
  16.9 34.0 %all-gather.2.cloned.1.call-done = bf16[256,1,16,128]{3,0,2,1:T(8,128)(2,1)} async-done(((bf16[32,1,16,128]{3,0,2,1:T(8,128)(2,1)}), bf16[256,1,16,128]{3,0,2,1:T(8,128)(2,1)}) %all-gather.2.cloned.1.call-update) | async-done | bytes 1048592 | tf_op jit(solution)/shard_map/all_gather | solution.py:59
  51.0 1.5 copy.17
  52.4 1.8 fusion.23
  54.2 1.8 fusion.105
  56.1 1.8 fusion.102
  57.9 1.9 fusion.99
  59.8 1.8 fusion.91
  61.7 1.3 pad_slice_fusion.1
  63.1 1.3 copy.94
  64.4 1.3 slice.199
  65.7 2.4 copy.93
  68.1 2.4 copy.95
  70.5 1.9 fusion.86
  72.4 1.8 fusion.81
  74.2 1.9 fusion.57
  76.1 2.0 fusion.56
  78.2 1.9 fusion.55
  80.1 1.9 fusion.54
  82.0 1.9 fusion.53
  84.0 1.9 fusion.52
  85.9 1.9 fusion.51
  87.8 1.9 fusion.50
  89.8 1.9 fusion.49
  92.7 1.0 fusion.47
  93.8 1.0 fusion.46
  95.8 1.0 fusion.44
  96.9 1.0 fusion.43
  98.9 1.0 fusion.41
  103.1 1.0 fusion.37
  106.2 1.0 fusion.34
  108.2 1.0 fusion.32
  109.3 1.0 fusion.31
  111.5 1.1 fusion.28
  113.6 1.1 fusion.27
  115.7 1.1 fusion.12
  116.8 1.2 fusion.11
  118.2 1.1 fusion.26
  119.3 7.8 %collective-permute-start = (bf16[256,16,128]{2,0,1:T(8,128)(2,1)S(1)}, bf16[256,16,128]{2,0,1:T(8,128)(2,1)S(1)}, u32[]{:S(2)}, u32[]{:S(2)}) collective-permute-start(bf16[256,16,128]{2,0,1:T(8,128)(2,1)S(1)} %bitcast.519), channel_id=1, source_target_pairs={{8,0},{16,8},{24,16},{32,24},{40,32},{48,40},{56,48},{64,56},{72,6... | collective-permute-start | bytes 3145736 | tf_op jit(solution)/shard_map/ppermute | solution.py:11
  127.2 1.8 fusion.9
  129.0 1.2 fusion.7
  130.2 1.1 fusion.5
  133.4 1.8 fusion.94
  135.2 1.1 fusion.4
  136.4 1.9 fusion.3
  138.2 237.4 %all-reduce.8.cloned.1.call-done = f32[27,32,256]{2,1,0:T(8,128)} async-done(((f32[27,32,256]{2,1,0:T(8,128)}), f32[27,32,256]{2,1,0:T(8,128)}) %all-reduce.8.cloned.1.call-update) | async-done | bytes 884752 | tf_op jit(solution)/shard_map/psum | solution.py:98
  375.6 2.2 broadcast_multiply_fusion
  377.8 1.3 slice.201
  379.2 1.3 copy.96
  380.5 1.3 concatenate.31.clone
  381.8 1.8 convolution_bitcast_fusion.6
  383.7 1.8 convolution_bitcast_fusion.1
  385.5 2.4 copy.51
  387.9 1.3 concatenate.30.clone
  389.2 1.8 convolution_bitcast_fusion.8
  391.0 1.8 convolution_bitcast_fusion.2
  393.8 1.4 fusion.25
  396.1 1.1 fusion.30
  398.3 1.1 fusion.29
  401.2 1.1 fusion.2
  402.3 1.1 fusion.24
  406.5 2.6 copy.41
  (91 shorter events, 24.2 us)
Async XLA Ops:
  7.2 43.8 %all-gather.2.cloned.1.call-start = ((), (), s32[]{:S(2)}) async-start(), calls=%async_computation | async-start | bytes 1179648 | tf_op jit(solution)/shard_map/all_gather | solution.py:59
  8.8 1.0 slice-start
  8.8 7.1 %copy-start.6 = (bf16[32,1,8,16,128]{4,3,2,1,0:T(8,128)(2,1)S(1)}, bf16[32,1,8,16,128]{4,3,2,1,0:T(8,128)(2,1)}, u32[]{:S(2)}) copy-start(bf16[32,1,8,16,128]{4,3,2,1,0:T(8,128)(2,1)} %param.3) | copy-start | bytes 3145732
  8.9 366.8 %all-reduce.8.cloned.1.call-start = ((), (), s32[]{:S(2)}) async-start(), calls=%async_computation.1 | async-start | bytes 1769472 | tf_op jit(solution)/shard_map/psum | solution.py:98
  11.0 63.2 %collective-permute-start.1 = (bf16[32,1,4,16,128]{4,0,3,2,1:T(8,128)(2,1)}, bf16[32,1,4,16,128]{4,0,3,2,1:T(8,128)(2,1)}, u32[]{:S(2)}, u32[]{:S(2)}) collective-permute-start(bf16[32,1,4,16,128]{4,0,3,2,1:T(8,128)(2,1)} %copy.42), channel_id=1, source_target_pairs={{0,8},{8,16},{16,24},{24,32},{32,40},{40,48},{48,56},{56,64},{64,7... | collective-permute-start | bytes 1572872 | tf_op jit(solution)/shard_map/ppermute | solution.py:11
  57.9 3.8 copy-start
  70.4 3.8 copy-start.2
  76.1 4.0 copy-start.1
  91.7 1.0 copy-start.8
  93.8 1.0 copy-start.9
  94.8 1.0 copy-start.23
  103.1 1.0 copy-start.7
  104.1 1.0 copy-start.22
  109.3 1.2 copy-start.4
  110.5 0.9 copy-start.16
  110.6 2.0 copy-start.5
  112.6 1.0 copy-start.15
  114.7 1.0 copy-start.13
  116.8 1.3 copy-start.3
  119.3 7.9 %copy-start.10 = (f32[32,2048]{1,0:T(8,128)S(1)}, f32[32,2048]{1,0:T(8,128)}, u32[]{:S(2)}) copy-start(f32[32,2048]{1,0:T(8,128)} %fusion.91) | copy-start | bytes 786436
  119.3 9.7 %copy-start.12 = (f32[32,2048]{1,0:T(8,128)S(1)}, f32[32,2048]{1,0:T(8,128)}, u32[]{:S(2)}) copy-start(f32[32,2048]{1,0:T(8,128)} %fusion.86) | copy-start | bytes 786436
  119.3 258.4 %collective-permute-start = (bf16[256,16,128]{2,0,1:T(8,128)(2,1)S(1)}, bf16[256,16,128]{2,0,1:T(8,128)(2,1)S(1)}, u32[]{:S(2)}, u32[]{:S(2)}) collective-permute-start(bf16[256,16,128]{2,0,1:T(8,128)(2,1)S(1)} %bitcast.519), channel_id=1, source_target_pairs={{8,0},{16,8},{24,16},{32,24},{40,32},{48,40},{56,48},{64,56},{72,6... | collective-permute-start | bytes 3145736 | tf_op jit(solution)/shard_map/ppermute | solution.py:11
  129.0 1.2 copy-start.11
  393.7 1.5 copy-start.19
  395.2 1.0 copy-start.14
  397.3 1.0 copy-start.18
  400.1 1.0 copy-start.17
  400.1 1.0 copy-start.20
  400.1 1.1 copy-start.21
  403.5 0.9 copy-start.24
Sparse Core Ops, SparseCore 0:
  10.4 40.5 all-gather.1
  110.5 265.1 all-reduce.7
where the time goes:
time: 419 us; the launch traced here: 416 us
  waiting for transfers between devices  271 us (65%)
  matrix products  77 us (18%)
  local copies, waits for them, and re-layouts  38 us (9%)
  between operations  14.5 us (3%)
  starting transfers between devices  12.8 us (3%)
    psum x1, waiting for transfers between devices, on_device(): grad_weight = lax.psum(grad_w, 'grid') * scale_norm  237 us
    dot_general x27, matrix products, on_device(): jnp.dot(weight[tap_x * 9 + tap_y * 3 + tap_z], window, preferred_element_...  40.9 us
    dot_general x27, matrix products, on_device(): jnp.einsum('cxyz,oxyz->co', act_slab, grad_slab, preferred_element_type=j...  36.1 us
    all_gather x1, waiting for transfers between devices, on_device(): gathered = lax.all_gather(grad_out, 'chan', axis=0, tiled=True)  34 us
    unnamed x72, local copies, waits for them, and re-layouts  25.9 us
    ppermute x2, starting transfers between devices, shifted_2(): return lax.ppermute(block, axis, route)  12.7 us
  transfers between devices with their start and end apart: 4, of which 2 were waited for; matrix products, arithmetic and copies ran while one was open for 11% of the time, Pallas kernels for 0%

commit v1 on v0

--- a/solution.py
+++ b/solution.py
@@ -3,6 +3,7 @@
 import jax.numpy as jnp
 from jax import lax
 from jax.sharding import PartitionSpec as P
+from jax.lax import all_gather
 
 
 def shifted_2(block, axis, distance):
@@ -95,7 +96,7 @@
     grad_w = tap_terms
     totals, grad_w = (totals, grad_w)
     grad_act = totals.astype(jnp.bfloat16)
-    grad_weight = lax.psum(grad_w, "grid") * scale_norm
+    grad_weight = all_gather(grad_w, axis_name="grid").sum(axis=0) * scale_norm
     return (grad_act, grad_weight)
 
 

time: 419 us -> 332 us (0.79)
  waiting for transfers between devices: 271 us -> 171 us
  other arithmetic: 2.17 us -> 11.2 us
    psum x1 -> x0, waiting for transfers between devices: 237 us -> none  [on_device(): grad_weight = lax.psum(grad_w, 'grid') * scale_norm]
    all_gather x0 -> x1, waiting for transfers between devices: none -> 120 us  [on_device(): grad_weight = all_gather(grad_w, axis_name='grid').sum(axis=0) * scale_norm]
    ppermute x2, waiting for transfers between devices: 0.01 us -> 19.1 us  [shifted_2(): return lax.ppermute(block, axis, route)]
    reduce_sum x0 -> x1, other arithmetic: none -> 10.2 us  [on_device(): grad_weight = all_gather(grad_w, axis_name='grid').sum(axis=0) * scale_norm]
    dot_general x27, matrix products: 36.1 us -> 44.7 us  [on_device(): jnp.einsum('cxyz,oxyz->co', act_slab, grad_slab, preferred_element_type=j...]
    dot_general x27, matrix products: 40.9 us -> 33.6 us  [on_device(): jnp.dot(weight[tap_x * 9 + tap_y * 3 + tap_z], window, preferred_element_...]
    unnamed x72 -> x36, local copies, waits for them, and re-layouts: 25.9 us -> 20.3 us
  transfers between devices with their start and end apart: 4 -> 4, of which waited for: 2 -> 3; matrix products, arithmetic and copies ran while one was open for 11% -> 22% of each run, Pallas kernels for 0% -> 0%
where the time goes in v1:
time: 332 us; the launch traced here: 329 us
  waiting for transfers between devices  171 us (52%)
  matrix products  78.2 us (24%)
  local copies, waits for them, and re-layouts  40.9 us (12%)
  between operations  14.3 us (4%)
  starting transfers between devices  12.8 us (4%)
  other arithmetic  11.2 us (3%)
    all_gather x1, waiting for transfers between devices, on_device(): grad_weight = all_gather(grad_w, axis_name='grid').sum(axis=0) * scale_norm  120 us
    dot_general x27, matrix products, on_device(): jnp.einsum('cxyz,oxyz->co', act_slab, grad_slab, preferred_element_type=j...  44.7 us
    dot_general x27, matrix products, on_device(): jnp.dot(weight[tap_x * 9 + tap_y * 3 + tap_z], window, preferred_element_...  33.6 us
    all_gather x1, waiting for transfers between devices, on_device(): gathered = lax.all_gather(grad_out, 'chan', axis=0, tiled=True)  32.8 us
    unnamed x36, local copies, waits for them, and re-layouts  20.3 us
    ppermute x2, waiting for transfers between devices, shifted_2(): return lax.ppermute(block, axis, route)  19.1 us
    ppermute x2, starting transfers between devices, shifted_2(): return lax.ppermute(block, axis, route)  12.7 us
    reduce_sum x1, other arithmetic, on_device(): grad_weight = all_gather(grad_w, axis_name='grid').sum(axis=0) * scale_norm  10.2 us
  transfers between devices with their start and end apart: 4, of which 3 were waited for; matrix products, arithmetic and copies ran while one was open for 22% of the time, Pallas kernels for 0%

profile of v1, /device:TPU:1, one launch (start us, length us, event | category | flops | bytes accessed | tf_op | source)
XLA Modules:
  0.0 328.9 jit_solution(13872411936002487124)
XLA Ops:
  7.2 1.6 copy.42
  10.0 1.1 copy.68
  11.1 4.9 %collective-permute-start.1 = (bf16[32,1,4,16,128]{4,0,3,2,1:T(8,128)(2,1)}, bf16[32,1,4,16,128]{4,0,3,2,1:T(8,128)(2,1)}, u32[]{:S(2)}, u32[]{:S(2)}) collective-permute-start(bf16[32,1,4,16,128]{4,0,3,2,1:T(8,128)(2,1)} %copy.68), channel_id=1, source_target_pairs={{0,8},{8,16},{16,24},{24,32},{32,40},{40,48},{48,56},{56,64},{64,7... | collective-permute-start | bytes 1572872 | tf_op jit(solution)/shard_map/ppermute | solution.py:12
  16.0 2.2 fusion.162
  18.3 32.8 %all-gather.4.cloned.1.call-done = bf16[256,1,16,128]{3,0,2,1:T(8,128)(2,1)} async-done(((bf16[32,1,16,128]{3,0,2,1:T(8,128)(2,1)}), bf16[256,1,16,128]{3,0,2,1:T(8,128)(2,1)}) %all-gather.4.cloned.1.call-update) | async-done | bytes 1048592 | tf_op jit(solution)/shard_map/all_gather | solution.py:60
  51.0 1.7 slice.199
  52.7 1.3 slice.200
  54.4 2.1 fusion.57
  56.5 1.9 fusion.56
  58.4 1.9 fusion.55
  60.3 1.9 fusion.54
  62.3 2.3 fusion.53
  64.6 2.3 fusion.52
  66.9 1.9 fusion.51
  68.9 2.3 fusion.50
  71.2 2.3 fusion.49
  74.6 1.9 fusion.47
  77.5 1.9 fusion.45
  79.5 2.3 fusion.44
  81.8 2.3 fusion.43
  85.2 2.3 fusion.41
  87.5 2.3 fusion.40
  99.1 1.4 copy.119
  100.5 1.3 copy.120
  101.8 2.4 copy.121
  104.2 1.3 concatenate.27.clone
  107.2 1.1 fusion.28
  108.4 1.3 concatenate.28.clone
  109.7 1.1 fusion.102
  110.8 1.1 fusion.27
  112.0 1.3 concatenate.29.clone
  114.4 1.1 fusion.12
  115.5 1.1 fusion.11
  116.7 1.2 fusion.26
  117.9 7.8 %collective-permute-start = (bf16[256,16,128]{2,0,1:T(8,128)(2,1)S(1)}, bf16[256,16,128]{2,0,1:T(8,128)(2,1)S(1)}, u32[]{:S(2)}, u32[]{:S(2)}) collective-permute-start(bf16[256,16,128]{2,0,1:T(8,128)(2,1)S(1)} %bitcast.520), channel_id=1, source_target_pairs={{8,0},{16,8},{24,16},{32,24},{40,32},{48,40},{56,48},{64,56},{72,6... | collective-permute-start | bytes 3145736 | tf_op jit(solution)/shard_map/ppermute | solution.py:12
  125.6 1.1 fusion.23
  126.9 1.9 fusion.94
  128.8 1.1 fusion.91
  129.9 1.1 fusion.86
  131.1 1.9 fusion.9
  134.1 1.1 fusion.81
  135.2 1.1 fusion.5
  136.3 1.1 fusion.4
  137.5 1.8 fusion.3
  139.3 19.1 %collective-permute-done = bf16[256,16,128]{2,0,1:T(8,128)(2,1)S(1)} collective-permute-done((bf16[256,16,128]{2,0,1:T(8,128)(2,1)S(1)}, bf16[256,16,128]{2,0,1:T(8,128)(2,1)S(1)}, u32[]{:S(2)}, u32[]{:S(2)}) %collective-permute-start) | collective-permute-done | bytes 1048608 | tf_op jit(solution)/shard_map/ppermute | solution.py:12
  159.5 1.8 copy.47
  161.4 1.4 fusion.25
  162.8 1.4 copy.77
  164.2 1.3 concatenate.30.clone
  166.6 1.4 fusion.30
  168.7 1.3 copy.122
  170.0 1.3 concatenate.31.clone
  172.4 1.2 fusion.29
  173.6 2.5 pad_slice_fusion
  176.1 2.6 copy.78
  178.7 1.5 concatenate.32.clone
  180.2 1.1 convolution_bitcast_fusion.1
  181.3 1.1 convolution_bitcast_fusion.2
  182.5 1.4 fusion.2
  183.9 1.1 fusion.24
  185.7 1.6 copy_dynamic-update-slice_fusion.2
  188.7 2.6 copy.67
  191.3 119.5 %all-gather.6.cloned.1.call-done = f32[864,32,256]{2,1,0:T(8,128)} async-done(((f32[27,32,256]{2,1,0:T(8,128)}), f32[864,32,256]{2,1,0:T(8,128)}) %all-gather.6.cloned.1.call-update) | async-done | bytes 28311568 | tf_op jit(solution)/shard_map/all_gather | solution.py:99
  310.8 10.2 %reduce_sum.9 = f32[27,32,256]{2,1,0:T(8,128)S(1)} reduce(f32[32,27,32,256]{3,2,1,0:T(8,128)} %bitcast.528, f32[]{:T(128)} %constant.0.clone.1), dimensions={0}, to_apply=%region_0.0 | reduce | flops 6856704 | bytes 29196292 | tf_op jit(solution)/shard_map/reduce_sum | solution.py:99
  (55 shorter events, 25.1 us)
Async XLA Ops:
  7.2 43.9 %all-gather.4.cloned.1.call-start = ((), (), s32[]{:S(2)}) async-start(), calls=%async_computation | async-start | bytes 1179648 | tf_op jit(solution)/shard_map/all_gather | solution.py:60
  8.8 302.0 %all-gather.6.cloned.1.call-start = ((), (), s32[]{:S(2)}) async-start(), calls=%async_computation.1 | async-start | bytes 29196288 | tf_op jit(solution)/shard_map/all_gather | solution.py:99
  11.1 43.2 %collective-permute-start.1 = (bf16[32,1,4,16,128]{4,0,3,2,1:T(8,128)(2,1)}, bf16[32,1,4,16,128]{4,0,3,2,1:T(8,128)(2,1)}, u32[]{:S(2)}, u32[]{:S(2)}) collective-permute-start(bf16[32,1,4,16,128]{4,0,3,2,1:T(8,128)(2,1)} %copy.68), channel_id=1, source_target_pairs={{0,8},{8,16},{16,24},{24,32},{32,40},{40,48},{48,56},{56,64},{64,7... | collective-permute-start | bytes 1572872 | tf_op jit(solution)/shard_map/ppermute | solution.py:12
  51.0 41.8 %copy-start.5 = (bf16[32,1,1,16,128]{4,3,2,1,0:T(8,128)(2,1)S(1)}, bf16[32,1,1,16,128]{4,3,2,1,0:T(8,128)(2,1)}, u32[]{:S(2)}) copy-start(bf16[32,1,1,16,128]{4,3,2,1,0:T(8,128)(2,1)} %get-tuple-element.9) | copy-start | bytes 393220
  51.0 42.9 %copy-start = (bf16[256,1,16,128]{3,0,2,1:T(8,128)(2,1)S(1)}, bf16[256,1,16,128]{3,0,2,1:T(8,128)(2,1)}, u32[]{:S(2)}) copy-start(bf16[256,1,16,128]{3,0,2,1:T(8,128)(2,1)} %all-gather.4.cloned.1.call-done) | copy-start | bytes 3145732
  51.0 42.9 %copy-start.6 = (bf16[32,1,1,16,128]{4,3,2,1,0:T(8,128)(2,1)S(1)}, bf16[32,1,1,16,128]{4,3,2,1,0:T(8,128)(2,1)}, u32[]{:S(2)}) copy-start(bf16[32,1,1,16,128]{4,3,2,1,0:T(8,128)(2,1)} %get-tuple-element.8) | copy-start | bytes 393220
  54.3 35.4 %copy-start.1 = (bf16[256,1,16,127]{3,0,2,1:T(8,128)(2,1)}, bf16[256,1,16,127]{3,0,2,1:T(8,128)(2,1)S(1)}, u32[]{:S(2)}) copy-start(bf16[256,1,16,127]{3,0,2,1:T(8,128)(2,1)S(1)} %pad_slice_fusion.1) | copy-start | bytes 3121156
  117.9 40.6 %collective-permute-start = (bf16[256,16,128]{2,0,1:T(8,128)(2,1)S(1)}, bf16[256,16,128]{2,0,1:T(8,128)(2,1)S(1)}, u32[]{:S(2)}, u32[]{:S(2)}) collective-permute-start(bf16[256,16,128]{2,0,1:T(8,128)(2,1)S(1)} %bitcast.520), channel_id=1, source_target_pairs={{8,0},{16,8},{24,16},{32,24},{40,32},{48,40},{56,48},{64,56},{72,6... | collective-permute-start | bytes 3145736 | tf_op jit(solution)/shard_map/ppermute | solution.py:12
  126.9 31.5 %copy-start.4 = (bf16[32,1,8,16,128]{4,0,3,2,1:T(8,128)(2,1)}, bf16[32,1,8,16,128]{4,0,3,2,1:T(8,128)(2,1)S(1)}, u32[]{:S(2)}) copy-start(bf16[32,1,8,16,128]{4,0,3,2,1:T(8,128)(2,1)S(1)} %copy_dynamic-update-slice_fusion.4) | copy-start | bytes 3145732
  158.4 1.0 copy-start.2
  159.5 9.2 %copy-start.3 = (bf16[256,1,15,128]{3,0,2,1:T(8,128)(2,1)}, bf16[256,1,15,128]{3,0,2,1:T(8,128)(2,1)S(1)}, u32[]{:S(2)}) copy-start(bf16[256,1,15,128]{3,0,2,1:T(8,128)(2,1)S(1)} %slice.202) | copy-start | bytes 2949124
Sparse Core Ops, SparseCore 0:
  10.4 40.6 all-gather.3
  99.2 211.5 all-gather.5
